TPU v7x, 256 devices: a whole 4x4x8 slice. The times are simulated.
256 devices in a mesh: ep: 8 (over y, core), seq: 32 (over z, x).
Axes of the slice: x: 4, y: 4, z: 8, core: 2. Of those that a mesh axis runs over, the one named last changes fastest.
Arguments:
- frames: bfloat16 [8, 22528, 512], P('ep', 'seq'), may hold values from -6 to 6
- lengths: int32 [8], P('ep'), may hold values from 11264 to 22528
- w_in: bfloat16 [512, 1024], replicated, may hold values from -0.25 to 0.25
- kernel: float32 [31, 512], replicated, may hold values from -1 to 1
- w_out: bfloat16 [512, 512], replicated, may hold values from -0.25 to 0.25
- pool_query: bfloat16 [8, 512], replicated, may hold values from -600 to 600
- w_value: bfloat16 [512, 512], replicated, may hold values from -0.25 to 0.25
- text_emb: bfloat16 [256, 512], replicated, may hold values from -6 to 6
- teacher: float32 [8, 256], P('ep'), may hold values from -6 to 6
Outputs:
- loss: float32 [], replicated
- grad_in: float32 [512, 1024], P('seq', 'ep')
- grad_out: float32 [512, 512], P('seq', 'ep')
- grad_kernel: float32 [31, 512], replicated
- grad_query: float32 [8, 512], replicated
- grad_value: float32 [512, 512], replicated
All inputs are finite; a program needn't handle non-finite values.
Results may differ from a plain program's by a relative error of at most 0.03.
Values may be sent and summed in bfloat16 or wider, within the bound.
No kernel may reach another device: no remote copies, remote signals or barrier semaphores. Data moves between devices by JAX's collectives and lax.ppermute only.
A program may use at most 64 MiB of HBM per device.

v0:
```python
import jax
import jax.numpy as jnp
from jax import lax
from jax.sharding import PartitionSpec as P


def padded_2(block, sides, width):
    for axis, dim in sides:
        count = lax.axis_size(axis)
        forward = [(i, i + 1) for i in range(count - 1)]
        backward = [(target, source) for source, target in forward]
        low = lax.ppermute(
            lax.slice_in_dim(block, block.shape[dim] - width, None, axis=dim), axis, forward
        )
        high = lax.ppermute(lax.slice_in_dim(block, 0, width, axis=dim), axis, backward)
        block = jnp.concatenate([low, block, high], axis=dim)
    return block


def shards(frames, lengths, w_in, kernel, w_out, pool_query, w_value, text_emb, teacher):
    hi = lax.Precision.HIGHEST
    n_epis, n_rows, width = frames.shape
    n_taps = kernel.shape[0]
    rim = n_taps // 2
    n_heads = pool_query.shape[0]
    head_dim = width // n_heads
    n_cands = text_emb.shape[0]
    root_width = jnp.sqrt(jnp.float32(width))
    offset = lax.axis_index("seq") * n_rows
    positions = offset + jnp.arange(n_rows, dtype=jnp.int32)
    valid = (positions[None, :] < lengths[:, None]).astype(jnp.float32)[..., None]
    xf = frames.astype(jnp.float32)
    mean_val = jnp.mean(xf, axis=-1, keepdims=True)
    var_val = jnp.mean((xf - mean_val) ** 2, axis=-1, keepdims=True)
    normed = ((xf - mean_val) * lax.rsqrt(var_val + 1e-05)).astype(jnp.bfloat16)
    mixed = jnp.einsum("esd,df->esf", normed, w_in, preferred_element_type=jnp.float32)
    sig = jax.nn.sigmoid(mixed[..., width:])
    glu = (mixed[..., :width] * sig * valid).astype(jnp.bfloat16)
    padded = padded_2(glu, (("seq", 1),), rim)
    conv = jnp.zeros((n_epis, n_rows, width), jnp.float32)
    for k in range(n_taps):
        conv = conv + kernel[k] * padded[:, k : k + n_rows].astype(jnp.float32)
    sconv = jax.nn.sigmoid(conv)
    act = (conv * sconv).astype(jnp.bfloat16)
    resid = xf + jnp.einsum("esd,df->esf", act, w_out, preferred_element_type=jnp.float32)
    queries = pool_query.astype(jnp.float32)
    scores = jnp.einsum("esd,hd->esh", resid, queries, precision=hi) / root_width
    masked = jnp.where(valid > 0, scores, -1e30)
    top = lax.pmax(jnp.max(masked, axis=1), "seq")
    expo = jnp.where(valid > 0, jnp.exp(masked - top[:, None]), 0.0)
    vec_here = jnp.einsum("esh,esd->ehd", expo, resid, precision=hi)
    total, vec = lax.psum((jnp.sum(expo, axis=1), vec_here), "seq")
    probs = jnp.where(valid > 0, jnp.exp(masked - top[:, None]), 0.0) / total[:, None]
    vbar = vec / total[..., None]
    wvals = w_value.astype(jnp.float32).reshape(width, n_heads, head_dim)
    pooled = jnp.einsum("ehd,dhk->ehk", vbar, wvals, precision=hi).reshape(n_epis, width)
    rms = jnp.sqrt(jnp.mean(pooled * pooled, axis=-1, keepdims=True) + 1e-06)
    emb = pooled / rms
    texts = text_emb.astype(jnp.float32)
    score = jnp.einsum("ed,cd->ec", emb, texts, precision=hi) / root_width
    diff = score - teacher
    loss_here = jnp.sum(diff * diff) / n_cands
    dscore = 2.0 * diff / n_cands
    demb = jnp.einsum("ec,cd->ed", dscore, texts, precision=hi) / root_width
    dpooled = (demb - emb * jnp.mean(demb * emb, axis=-1, keepdims=True)) / rms
    dp3 = dpooled.reshape(n_epis, n_heads, head_dim)
    value_here = jnp.einsum("ehd,ehk->dhk", vbar, dp3, precision=hi).reshape(width, width)
    dvbar = jnp.einsum("dhk,ehk->ehd", wvals, dp3, precision=hi)
    proj = jnp.einsum("esd,ehd->esh", resid, dvbar, precision=hi)
    centre = jnp.sum(dvbar * vbar, axis=-1)
    dscores = probs * (proj - centre[:, None])
    query_here = jnp.einsum("esh,esd->hd", dscores, resid, precision=hi) / root_width
    dresid = (
        jnp.einsum("esh,ehd->esd", probs, dvbar, precision=hi)
        + jnp.einsum("esh,hd->esd", dscores, queries, precision=hi) / root_width
    ).astype(jnp.bfloat16)
    out_here = jnp.einsum("esd,esf->df", act, dresid, preferred_element_type=jnp.float32)
    dact = jnp.einsum("esf,df->esd", dresid, w_out, preferred_element_type=jnp.float32)
    dconv = (dact * sconv * (1.0 + conv * (1.0 - sconv))).astype(jnp.bfloat16)
    dconv_f = dconv.astype(jnp.float32)
    dpad = padded_2(dconv, (("seq", 1),), rim)
    dglu = jnp.zeros((n_epis, n_rows, width), jnp.float32)
    taps = []
    for k in range(n_taps):
        dglu = dglu + kernel[k] * dpad[:, 2 * rim - k : 2 * rim - k + n_rows].astype(jnp.float32)
        taps.append(jnp.sum(padded[:, k : k + n_rows].astype(jnp.float32) * dconv_f, axis=(0, 1)))
    kernel_here = jnp.stack(taps)
    dglu = dglu * valid
    dmixed = jnp.concatenate(
        [dglu * sig, dglu * mixed[..., :width] * sig * (1.0 - sig)], axis=-1
    ).astype(jnp.bfloat16)
    in_here = jnp.einsum("esd,esf->df", normed, dmixed, preferred_element_type=jnp.float32)
    rows_in, rows_out = (
        lax.psum_scatter(
            in_here.astype(jnp.bfloat16), "seq", scatter_dimension=0, tiled=True
        ).astype(jnp.float32),
        lax.psum_scatter(
            out_here.astype(jnp.bfloat16), "seq", scatter_dimension=0, tiled=True
        ).astype(jnp.float32),
    )
    grad_in, grad_out = (
        lax.psum_scatter(
            rows_in.astype(jnp.bfloat16), "ep", scatter_dimension=1, tiled=True
        ).astype(jnp.float32),
        lax.psum_scatter(
            rows_out.astype(jnp.bfloat16), "ep", scatter_dimension=1, tiled=True
        ).astype(jnp.float32),
    )
    grad_kernel, grad_query = lax.psum((kernel_here, query_here), ("ep", "seq"))
    grad_value, loss = (
        lax.psum(value_here.astype(jnp.bfloat16), "ep").astype(jnp.float32),
        lax.psum(loss_here.astype(jnp.bfloat16), "ep").astype(jnp.float32),
    )
    return (loss, grad_in, grad_out, grad_kernel, grad_query, grad_value)


def solution(mesh):
    return jax.shard_map(
        shards,
        mesh=mesh,
        in_specs=(P("ep", "seq", None), P("ep"), P(), P(), P(), P(), P(), P(), P("ep", None)),
        out_specs=(P(), P("seq", "ep"), P("seq", "ep"), P(), P(), P()),
        check_vma=False,
    )
```

profile of v0, /device:TPU:1, one launch (start us, length us, event | category | flops | bytes accessed | tf_op | source)
XLA Modules:
  0.0 1106.2 jit_solution(10548095060268716896)
XLA Ops:
  9.3 1.5 fusion.5
  14.0 3.9 collective-permute-start
  20.6 1.8 collective-permute-done.1
  22.6 9.4 fusion.36
  34.1 62.9 %pmax.7 = f32[8]{0:T(128)S(1)} all-reduce(f32[8]{0:T(128)S(1)} %get-tuple-element.101), channel_id=1, replica_groups=mesh['ep'=8,'seq'=32] {'seq'}, use_global_device_ids=true, to_apply=%region_3.4 | all-reduce | flops 8 | bytes 64 | tf_op jit(solution)/shard_map/pmax | solution.py:49
  98.5 111.0 %all-reduce.1 = (f32[1,8,512]{2,1,0:T(8,128)}, f32[8]{0:T(128)S(1)}) all-reduce(f32[1,8,512]{2,1,0:T(8,128)S(1)} %convolution_bitcast_fusion.3, f32[8]{0:T(128)} %fusion.164), channel_id=1, replica_groups=mesh['ep'=8,'seq'=32] {'seq'}, use_global_device_ids=true, to_apply=%region_4.5 | all-reduce | flops 4104 | bytes 32832 | tf_op jit(solution)/shard_map/psum | solution.py:52
  210.4 1.5 fusion.161
  219.9 1.4 fusion.191
  222.1 2.1 fusion.159
  224.3 2.0 fusion.94
  227.7 2.1 fusion.67
  232.4 4.2 collective-permute-start.3
  236.5 1.4 convolution_convert_fusion.1
  238.4 25.7 %fusion.96 = (bf16[704,512]{1,0:T(8,128)(2,1)S(1)}, f32[1,704,512]{2,1,0:T(8,128)S(1)}) fusion(f32[1,704,1024]{2,1,0:T(8,128)} %copy-done.3, f32[704]{0:T(1024)S(1)} %copy-done.15, bf16[1,704,512]{2,1,0:T(8,128)(2,1)} %copy-done.1, bf16[1,15,512]{2,1,0:T(8,128)(2,1)S(1)} %collective-permute-done.3, f32[512]{0:T(512)S(1)} %bitcast.173, f32[512]{0:T(512)S(1)} %bitcast.175, ...), kind=kLoop, calls=%fused_computation.235 | loop fusion | flops 67764224 | bytes 4422400 | tf_op jit(solution)/shard_map/concatenate | solution.py:89
  265.2 2.1 convolution_convert_fusion
  268.5 2.5 fusion.82
  271.1 1.7 fusion.84
  272.8 1.5 fusion.83
  274.3 216.4 %reduce-scatter.11.cloned.1.call-done = bf16[16,512]{1,0:T(8,128)(2,1)} async-done(((bf16[512,512]{1,0:T(8,128)(2,1)}), bf16[16,512]{1,0:T(8,128)(2,1)}) %reduce-scatter.11.cloned.1.call-update) | async-done | bytes 16400 | tf_op jit(solution)/shard_map/reduce_scatter | solution.py:97
  490.6 1.5 copy.28
  492.2 2.2 fusion.68
  494.4 213.8 %reduce-scatter.9.cloned.1.call-done = bf16[16,1024]{1,0:T(8,128)(2,1)} async-done(((bf16[512,1024]{1,0:T(8,128)(2,1)}), bf16[16,1024]{1,0:T(8,128)(2,1)}) %reduce-scatter.9.cloned.1.call-update) | async-done | bytes 32784 | tf_op jit(solution)/shard_map/reduce_scatter | solution.py:94
  708.2 1.6 copy.26
  709.9 1.4 convolution_multiply_fusion.2
  711.3 2.5 stack.127
  715.1 18.4 %psum.44 = bf16[]{:T(256)} all-reduce(bf16[]{:T(256)S(6)} %div.117), channel_id=1, replica_groups=mesh['ep'=8,'seq'=32] {'ep'}, use_global_device_ids=true, to_apply=%region_9.10 | all-reduce | flops 1 | bytes 4 | tf_op jit(solution)/shard_map/psum | solution.py:112
  734.2 44.1 %all-reduce.5.cloned.1.call-done = bf16[512,512]{0,1:T(8,128)(2,1)} async-done(((bf16[512,512]{0,1:T(8,128)(2,1)}), bf16[512,512]{0,1:T(8,128)(2,1)}) %all-reduce.5.cloned.1.call-update) | async-done | bytes 524304 | tf_op jit(solution)/shard_map/psum | solution.py:111
  778.2 2.2 copy.21
  780.4 32.0 %reduce-scatter.15.cloned.1.call-done = bf16[64,16]{1,0:T(8,128)(2,1)} async-done(((bf16[512,16]{1,0:T(8,128)(2,1)}), bf16[64,16]{1,0:T(8,128)(2,1)}) %reduce-scatter.15.cloned.1.call-update) | async-done | bytes 2064
  813.8 33.0 %reduce-scatter.13.cloned.1.call-done = bf16[128,16]{1,0:T(8,128)(2,1)} async-done(((bf16[1024,16]{1,0:T(8,128)(2,1)}), bf16[128,16]{1,0:T(8,128)(2,1)}) %reduce-scatter.13.cloned.1.call-update) | async-done | bytes 4112
  848.3 247.1 %all-reduce.7.cloned.1.call-done = (f32[31,512]{1,0:T(8,128)}, f32[8,512]{1,0:T(8,128)}) async-done(((f32[31,512]{1,0:T(8,128)}, f32[8,512]{1,0:T(8,128)}), (f32[31,512]{1,0:T(8,128)}, f32[8,512]{1,0:T(8,128)})) %all-reduce.7.cloned.1.call-update) | async-done | bytes 79888 | tf_op jit(solution)/shard_map/psum | solution.py:109
  1095.4 1.5 copy.45
  (239 shorter events, 29.7 us)
Async XLA Ops:
  7.2 483.4 %reduce-scatter.11.cloned.1.call-start = ((), (), s32[]{:S(2)}) async-start(), calls=%async_computation.5 | async-start | bytes 540672 | tf_op jit(solution)/shard_map/reduce_scatter | solution.py:97
  12.4 6.8 copy-start.13
  12.4 7.2 copy-start.11
  14.0 6.7 collective-permute-start
  17.9 4.5 collective-permute-start.1
  19.3 12.7 %copy-start.22 = (f32[1,512]{1,0:T(1,128)}, f32[1,512]{1,0:T(1,128)S(1)}, u32[]{:S(2)}) copy-start(f32[1,512]{1,0:T(1,128)S(1)} %get-tuple-element.89) | copy-start | bytes 6148
  19.3 12.7 %copy-start.24 = (f32[1,512]{1,0:T(1,128)}, f32[1,512]{1,0:T(1,128)S(1)}, u32[]{:S(2)}) copy-start(f32[1,512]{1,0:T(1,128)S(1)} %get-tuple-element.90) | copy-start | bytes 6148
  19.4 12.7 %copy-start.26 = (f32[1,512]{1,0:T(1,128)}, f32[1,512]{1,0:T(1,128)S(1)}, u32[]{:S(2)}) copy-start(f32[1,512]{1,0:T(1,128)S(1)} %get-tuple-element.91) | copy-start | bytes 6148
  20.6 11.5 %copy-start.6 = (bf16[1,704,512]{2,1,0:T(8,128)(2,1)S(1)}, bf16[1,704,512]{2,1,0:T(8,128)(2,1)}, u32[]{:S(2)}) copy-start(bf16[1,704,512]{2,1,0:T(8,128)(2,1)} %param.9) | copy-start | bytes 2162692
  20.6 11.5 %copy-start.90 = (bf16[512,512]{1,0:T(8,128)(2,1)S(1)}, bf16[512,512]{1,0:T(8,128)(2,1)}, u32[]{:S(2)}) copy-start(bf16[512,512]{1,0:T(8,128)(2,1)} %param.13) | copy-start | bytes 1572868
  34.1 181.2 %copy-start.10 = (bf16[256,512]{1,0:T(8,128)(2,1)S(1)}, bf16[256,512]{1,0:T(8,128)(2,1)}, u32[]{:S(2)}) copy-start(bf16[256,512]{1,0:T(8,128)(2,1)} %param.16) | copy-start | bytes 786436
  209.5 11.7 %copy-start.12 = (f32[1,8,512]{2,1,0:T(8,128)S(1)}, f32[1,8,512]{2,1,0:T(8,128)}, u32[]{:S(2)}) copy-start(f32[1,8,512]{2,1,0:T(8,128)} %get-tuple-element.60) | copy-start | bytes 49156
  230.8 7.3 collective-permute-start.2
  232.0 6.0 copy-start.15
  232.1 6.0 copy-start.19
  232.1 6.0 copy-start.21
  232.1 6.0 copy-start.23
  232.1 6.0 copy-start.25
  232.1 6.0 copy-start.27
  232.1 6.0 copy-start.29
  232.1 6.0 copy-start.31
  232.1 6.0 copy-start.33
  232.1 6.0 copy-start.35
  232.4 5.7 collective-permute-start.3
  238.0 470.2 %reduce-scatter.9.cloned.1.call-start = ((), (), s32[]{:S(2)}) async-start(), calls=%async_computation.4 | async-start | bytes 1081344 | tf_op jit(solution)/shard_map/reduce_scatter | solution.py:94
  238.1 26.0 %copy-start.4 = (f32[1,704,1024]{2,1,0:T(8,128)S(1)}, f32[1,704,1024]{2,1,0:T(8,128)}, u32[]{:S(2)}) copy-start(f32[1,704,1024]{2,1,0:T(8,128)} %copy-done.3) | copy-start | bytes 8650756
  267.4 510.9 %all-reduce.5.cloned.1.call-start = ((), (), s32[]{:S(2)}) async-start(), calls=%async_computation.6 | async-start | bytes 1048576 | tf_op jit(solution)/shard_map/psum | solution.py:111
  268.5 544.0 %reduce-scatter.15.cloned.1.call-start = ((), (), s32[]{:S(2)}) async-start(), calls=%async_computation.8 | async-start | bytes 147456
  492.1 354.7 %reduce-scatter.13.cloned.1.call-start = ((), (), s32[]{:S(2)}) async-start(), calls=%async_computation.7 | async-start | bytes 294912
  494.4 219.4 %copy-start.84 = (f32[256]{0:T(256)S(1)}, f32[256]{0:T(256)}, u32[]{:S(2)}) copy-start(f32[256]{0:T(256)} %copy-done.83) | copy-start | bytes 3076
  494.4 219.4 %copy-start.87 = (f32[1,256]{1,0:T(1,128)S(1)}, f32[1,256]{1,0:T(1,128)}, u32[]{:S(2)}) copy-start(f32[1,256]{1,0:T(1,128)} %param.17) | copy-start | bytes 3076
  709.8 385.6 %all-reduce.7.cloned.1.call-start = ((), (), s32[]{:S(2)}) async-start(), calls=%async_computation.9 | async-start | bytes 163840 | tf_op jit(solution)/shard_map/psum | solution.py:109
  (70 other events, 251.9 us)
Sparse Core Ops, SparseCore 0:
  238.1 252.4 reduce-scatter.10
  495.5 212.6 reduce-scatter.8
  710.6 67.5 all-reduce.4
  780.6 31.8 reduce-scatter.14
  814.9 31.8 reduce-scatter.12
  852.8 242.5 all-reduce.6
where the time goes:
time: 1110 us
  waiting for transfers between devices  788 us (71%)
  blocking collectives  192 us (17%)
  other arithmetic  55.3 us (5%)
  between operations  20.1 us (2%)
  matrix products  20 us (2%)
  local copies, waits for them, and re-layouts  19.4 us (2%)
    psum x1, waiting for transfers between devices, shards(): grad_kernel, grad_query = lax.psum((kernel_here, query_here), ('ep', 'seq'))  247 us
    reduce_scatter x1, waiting for transfers between devices, shards(): lax.psum_scatter(out_here.astype(jnp.bfloat16), 'seq', scatter_dimension=...  216 us
    reduce_scatter x1, waiting for transfers between devices, shards(): lax.psum_scatter(in_here.astype(jnp.bfloat16), 'seq', scatter_dimension=0...  214 us
    psum x1, blocking collectives, shards(): total, vec = lax.psum((jnp.sum(expo, axis=1), vec_here), 'seq')  111 us
    unnamed x8, waiting for transfers between devices  65.1 us
    pmax x1, blocking collectives, shards(): top = lax.pmax(jnp.max(masked, axis=1), 'seq')  62.9 us
    psum x1, waiting for transfers between devices, shards(): lax.psum(value_here.astype(jnp.bfloat16), 'ep').astype(jnp.float32)  44.1 us
    concatenate x2, other arithmetic, shards(): jnp.concatenate([dglu * sig, dglu * mixed[..., :width] * sig * (1.0 - sig...  26.3 us
  transfers between devices with their start and end apart: 10, of which 7 were waited for; matrix products, arithmetic and copies ran while one was open for 5% of the time, Pallas kernels for 0%

commit v1 on v0

--- a/solution.py
+++ b/solution.py
@@ -106,7 +106,7 @@
             rows_out.astype(jnp.bfloat16), "ep", scatter_dimension=1, tiled=True
         ).astype(jnp.float32),
     )
-    grad_kernel, grad_query = lax.psum((kernel_here, query_here), ("ep", "seq"))
+    grad_kernel, grad_query = lax.psum(lax.psum((kernel_here, query_here), "seq"), "ep")
     grad_value, loss = (
         lax.psum(value_here.astype(jnp.bfloat16), "ep").astype(jnp.float32),
         lax.psum(loss_here.astype(jnp.bfloat16), "ep").astype(jnp.float32),

time: 1110 us -> 1070 us (0.964)
  waiting for transfers between devices: 788 us -> 748 us
    psum x1 -> x2, waiting for transfers between devices: 247 us -> 205 us  [the longest x1 142 us: shards(): lax.psum((kernel_here, query_here), 'seq')]
    unnamed x8 -> x9, waiting for transfers between devices: 65.1 us -> 65.1 us
  transfers between devices with their start and end apart: 10 -> 11, of which waited for: 7 -> 8; matrix products, arithmetic and copies ran while one was open for 5% -> 5% of each run, Pallas kernels for 0% -> 0%
where the time goes in v1:
time: 1070 us; the launch traced here: 1060 us
  waiting for transfers between devices  748 us (70%)
  blocking collectives  192 us (18%)
  other arithmetic  54.3 us (5%)
  between operations  20.1 us (2%)
  matrix products  20 us (2%)
  local copies, waits for them, and re-layouts  19.4 us (2%)
  starting transfers between devices  11 us (1%)
    reduce_scatter x1, waiting for transfers between devices, shards(): lax.psum_scatter(in_here.astype(jnp.bfloat16), 'seq', scatter_dimension=0...  216 us
    reduce_scatter x1, waiting for transfers between devices, shards(): lax.psum_scatter(out_here.astype(jnp.bfloat16), 'seq', scatter_dimension=...  211 us
    psum x1, waiting for transfers between devices, shards(): lax.psum((kernel_here, query_here), 'seq')  142 us
    psum x1, blocking collectives, shards(): total, vec = lax.psum((jnp.sum(expo, axis=1), vec_here), 'seq')  111 us
    unnamed x9, waiting for transfers between devices  65.1 us
    psum x1, waiting for transfers between devices, shards(): lax.psum(lax.psum((kernel_here, query_here), 'seq'), 'ep')  62.9 us
    pmax x1, blocking collectives, shards(): top = lax.pmax(jnp.max(masked, axis=1), 'seq')  62.9 us
    psum x1, waiting for transfers between devices, shards(): lax.psum(value_here.astype(jnp.bfloat16), 'ep').astype(jnp.float32)  48.5 us
  transfers between devices with their start and end apart: 11, of which 8 were waited for; matrix products, arithmetic and copies ran while one was open for 5% of the time, Pallas kernels for 0%

profile of v1, /device:TPU:1, one launch (start us, length us, event | category | flops | bytes accessed | tf_op | source)
XLA Modules:
  0.0 1064.4 jit_solution(3274245606193347924)
XLA Ops:
  9.3 1.5 fusion.5
  14.0 3.9 collective-permute-start
  20.6 1.8 collective-permute-done.1
  22.6 9.4 fusion.36
  34.1 62.9 %pmax.7 = f32[8]{0:T(128)S(1)} all-reduce(f32[8]{0:T(128)S(1)} %get-tuple-element.103), channel_id=1, replica_groups=mesh['ep'=8,'seq'=32] {'seq'}, use_global_device_ids=true, to_apply=%region_3.4 | all-reduce | flops 8 | bytes 64 | tf_op jit(solution)/shard_map/pmax | solution.py:49
  98.5 111.0 %all-reduce.1 = (f32[1,8,512]{2,1,0:T(8,128)}, f32[8]{0:T(128)S(1)}) all-reduce(f32[1,8,512]{2,1,0:T(8,128)S(1)} %convolution_bitcast_fusion.3, f32[8]{0:T(128)} %fusion.164), channel_id=1, replica_groups=mesh['ep'=8,'seq'=32] {'seq'}, use_global_device_ids=true, to_apply=%region_4.5 | all-reduce | flops 4104 | bytes 32832 | tf_op jit(solution)/shard_map/psum | solution.py:52
  210.4 1.5 fusion.161
  222.1 2.1 fusion.159
  224.3 2.0 fusion.94
  227.7 2.1 fusion.67
  232.4 4.2 collective-permute-start.3
  236.5 1.4 convolution_convert_fusion.1
  238.5 25.7 %fusion.96 = (bf16[704,512]{1,0:T(8,128)(2,1)S(1)}, f32[1,704,512]{2,1,0:T(8,128)S(1)}) fusion(f32[1,704,1024]{2,1,0:T(8,128)} %copy-done.3, f32[704]{0:T(1024)S(1)} %copy-done.15, bf16[1,704,512]{2,1,0:T(8,128)(2,1)} %copy-done.1, bf16[1,15,512]{2,1,0:T(8,128)(2,1)S(1)} %collective-permute-done.3, f32[512]{0:T(512)S(1)} %bitcast.173, f32[512]{0:T(512)S(1)} %bitcast.175, ...), kind=kLoop, calls=%fused_computation.235 | loop fusion | flops 67764224 | bytes 4422400 | tf_op jit(solution)/shard_map/concatenate | solution.py:89
  265.3 2.1 convolution_convert_fusion
  267.5 2.3 fusion.68
  269.8 1.5 fusion.82
  271.3 1.5 fusion.83
  272.8 1.7 fusion.84
  274.5 2.5 stack.127
  277.0 1.4 convolution_multiply_fusion.2
  279.5 211.2 %reduce-scatter.11.cloned.1.call-done = bf16[16,512]{1,0:T(8,128)(2,1)} async-done(((bf16[512,512]{1,0:T(8,128)(2,1)}), bf16[16,512]{1,0:T(8,128)(2,1)}) %reduce-scatter.11.cloned.1.call-update) | async-done | bytes 16400 | tf_op jit(solution)/shard_map/reduce_scatter | solution.py:97
  490.7 1.5 copy.28
  492.2 216.2 %reduce-scatter.9.cloned.1.call-done = bf16[16,1024]{1,0:T(8,128)(2,1)} async-done(((bf16[512,1024]{1,0:T(8,128)(2,1)}), bf16[16,1024]{1,0:T(8,128)(2,1)}) %reduce-scatter.9.cloned.1.call-update) | async-done | bytes 32784 | tf_op jit(solution)/shard_map/reduce_scatter | solution.py:94
  708.4 1.6 copy.26
  710.1 142.3 %all-reduce.9.cloned.1.call-done = (f32[31,512]{1,0:T(8,128)}, f32[8,512]{1,0:T(8,128)}) async-done(((f32[31,512]{1,0:T(8,128)}, f32[8,512]{1,0:T(8,128)}), (f32[31,512]{1,0:T(8,128)}, f32[8,512]{1,0:T(8,128)})) %all-reduce.9.cloned.1.call-update) | async-done | bytes 79888 | tf_op jit(solution)/shard_map/psum | solution.py:109
  853.7 17.8 %psum.58 = bf16[]{:T(256)} all-reduce(bf16[]{:T(256)S(6)} %div.117), channel_id=1, replica_groups=mesh['ep'=8,'seq'=32] {'ep'}, use_global_device_ids=true, to_apply=%region_9.10 | all-reduce | flops 1 | bytes 4 | tf_op jit(solution)/shard_map/psum | solution.py:112
  872.2 48.5 %all-reduce.7.cloned.1.call-done = bf16[512,512]{0,1:T(8,128)(2,1)} async-done(((bf16[512,512]{0,1:T(8,128)(2,1)}), bf16[512,512]{0,1:T(8,128)(2,1)}) %all-reduce.7.cloned.1.call-update) | async-done | bytes 524304 | tf_op jit(solution)/shard_map/psum | solution.py:111
  920.7 2.2 copy.21
  922.9 32.0 %reduce-scatter.15.cloned.1.call-done = bf16[64,16]{1,0:T(8,128)(2,1)} async-done(((bf16[512,16]{1,0:T(8,128)(2,1)}), bf16[64,16]{1,0:T(8,128)(2,1)}) %reduce-scatter.15.cloned.1.call-update) | async-done | bytes 2064
  956.2 33.0 %reduce-scatter.13.cloned.1.call-done = bf16[128,16]{1,0:T(8,128)(2,1)} async-done(((bf16[1024,16]{1,0:T(8,128)(2,1)}), bf16[128,16]{1,0:T(8,128)(2,1)}) %reduce-scatter.13.cloned.1.call-update) | async-done | bytes 4112
  990.7 62.9 %all-reduce.11.cloned.1.call-done = (f32[31,512]{1,0:T(8,128)}, f32[8,512]{1,0:T(8,128)}) async-done(((f32[31,512]{1,0:T(8,128)}, f32[8,512]{1,0:T(8,128)}), (f32[31,512]{1,0:T(8,128)}, f32[8,512]{1,0:T(8,128)})) %all-reduce.11.cloned.1.call-update) | async-done | bytes 79888 | tf_op jit(solution)/shard_map/psum | solution.py:109
  1053.6 1.5 copy.47
  (242 shorter events, 31.1 us)
Async XLA Ops:
  7.2 483.5 %reduce-scatter.11.cloned.1.call-start = ((), (), s32[]{:S(2)}) async-start(), calls=%async_computation.5 | async-start | bytes 540672 | tf_op jit(solution)/shard_map/reduce_scatter | solution.py:97
  12.4 6.8 copy-start.13
  12.4 7.2 copy-start.11
  14.0 6.7 collective-permute-start
  17.9 4.5 collective-permute-start.1
  19.3 12.7 %copy-start.22 = (f32[1,512]{1,0:T(1,128)}, f32[1,512]{1,0:T(1,128)S(1)}, u32[]{:S(2)}) copy-start(f32[1,512]{1,0:T(1,128)S(1)} %get-tuple-element.91) | copy-start | bytes 6148
  19.3 12.7 %copy-start.24 = (f32[1,512]{1,0:T(1,128)}, f32[1,512]{1,0:T(1,128)S(1)}, u32[]{:S(2)}) copy-start(f32[1,512]{1,0:T(1,128)S(1)} %get-tuple-element.92) | copy-start | bytes 6148
  19.4 12.7 %copy-start.26 = (f32[1,512]{1,0:T(1,128)}, f32[1,512]{1,0:T(1,128)S(1)}, u32[]{:S(2)}) copy-start(f32[1,512]{1,0:T(1,128)S(1)} %get-tuple-element.93) | copy-start | bytes 6148
  20.6 11.5 %copy-start.6 = (bf16[1,704,512]{2,1,0:T(8,128)(2,1)S(1)}, bf16[1,704,512]{2,1,0:T(8,128)(2,1)}, u32[]{:S(2)}) copy-start(bf16[1,704,512]{2,1,0:T(8,128)(2,1)} %param.9) | copy-start | bytes 2162692
  20.6 11.5 %copy-start.90 = (bf16[512,512]{1,0:T(8,128)(2,1)S(1)}, bf16[512,512]{1,0:T(8,128)(2,1)}, u32[]{:S(2)}) copy-start(bf16[512,512]{1,0:T(8,128)(2,1)} %param.13) | copy-start | bytes 1572868
  34.1 181.2 %copy-start.10 = (bf16[256,512]{1,0:T(8,128)(2,1)S(1)}, bf16[256,512]{1,0:T(8,128)(2,1)}, u32[]{:S(2)}) copy-start(bf16[256,512]{1,0:T(8,128)(2,1)} %param.16) | copy-start | bytes 786436
  209.5 11.7 %copy-start.12 = (f32[1,8,512]{2,1,0:T(8,128)S(1)}, f32[1,8,512]{2,1,0:T(8,128)}, u32[]{:S(2)}) copy-start(f32[1,8,512]{2,1,0:T(8,128)} %get-tuple-element.60) | copy-start | bytes 49156
  230.8 7.4 collective-permute-start.2
  232.0 6.1 copy-start.15
  232.1 6.1 copy-start.19
  232.1 6.1 copy-start.21
  232.1 6.1 copy-start.23
  232.1 6.1 copy-start.25
  232.1 6.1 copy-start.27
  232.1 6.1 copy-start.29
  232.1 6.1 copy-start.31
  232.1 6.1 copy-start.33
  232.4 5.8 collective-permute-start.3
  238.1 470.4 %reduce-scatter.9.cloned.1.call-start = ((), (), s32[]{:S(2)}) async-start(), calls=%async_computation.4 | async-start | bytes 1081344 | tf_op jit(solution)/shard_map/reduce_scatter | solution.py:94
  238.1 26.0 %copy-start.4 = (f32[1,704,1024]{2,1,0:T(8,128)S(1)}, f32[1,704,1024]{2,1,0:T(8,128)}, u32[]{:S(2)}) copy-start(f32[1,704,1024]{2,1,0:T(8,128)} %copy-done.3) | copy-start | bytes 8650756
  267.4 584.9 %all-reduce.9.cloned.1.call-start = ((), (), s32[]{:S(2)}) async-start(), calls=%async_computation.9 | async-start | bytes 163840 | tf_op jit(solution)/shard_map/psum | solution.py:109
  277.0 575.4 %copy-start.84 = (f32[256]{0:T(256)S(1)}, f32[256]{0:T(256)}, u32[]{:S(2)}) copy-start(f32[256]{0:T(256)} %copy-done.83) | copy-start | bytes 3076
  277.0 575.4 %copy-start.87 = (f32[1,256]{1,0:T(1,128)S(1)}, f32[1,256]{1,0:T(1,128)}, u32[]{:S(2)}) copy-start(f32[1,256]{1,0:T(1,128)} %param.17) | copy-start | bytes 3076
  278.5 642.2 %all-reduce.7.cloned.1.call-start = ((), (), s32[]{:S(2)}) async-start(), calls=%async_computation.6 | async-start | bytes 1048576 | tf_op jit(solution)/shard_map/psum | solution.py:111
  279.5 675.4 %reduce-scatter.15.cloned.1.call-start = ((), (), s32[]{:S(2)}) async-start(), calls=%async_computation.8 | async-start | bytes 147456
  492.2 497.1 %reduce-scatter.13.cloned.1.call-start = ((), (), s32[]{:S(2)}) async-start(), calls=%async_computation.7 | async-start | bytes 294912
  710.1 343.6 %all-reduce.11.cloned.1.call-start = ((), (), s32[]{:S(2)}) async-start(), calls=%async_computation.10 | async-start | bytes 163840 | tf_op jit(solution)/shard_map/psum | solution.py:109
  (71 other events, 259.5 us)
Sparse Core Ops, SparseCore 0:
  238.2 252.4 reduce-scatter.10
  495.6 212.8 reduce-scatter.8
  712.9 139.4 all-reduce.8
  854.7 65.9 all-reduce.6
  923.0 31.8 reduce-scatter.14
  957.4 31.8 reduce-scatter.12
  991.7 61.9 all-reduce.10
